TPU v7x, 32 devices: a whole 2x2x4 slice. The times are simulated.
32 devices in a mesh: dp: 32 (over z, y, x, core).
Axes of the slice: x: 2, y: 2, z: 4, core: 2. Of those that a mesh axis runs over, the one named last changes fastest.
Arguments:
- hidden: bfloat16 [64, 512, 2048], P('dp'), may hold values from -6 to 6
- lengths: int32 [64], P('dp'), may hold values from 1 to 512, 16384 in all
- order: int32 [64], P('dp'), may hold values from 0 to 63, each once
- candidates: int32 [64, 64], replicated, may hold values from 0 to 16383, as said below
- norm_gain: float32 [2048], replicated, may hold values from 0.25 to 1.75
- w_query: bfloat16 [2048, 1024], P('dp'), may hold values from -1 to 1
- w_key: bfloat16 [2048, 1024], P('dp'), may hold values from -1 to 1
- w_value: bfloat16 [2048, 1024], P('dp'), may hold values from -0.125 to 0.125
- w_out: bfloat16 [1024, 2048], P('dp'), may hold values from -0.75 to 0.75
- index_rows: bfloat16 [16384, 2048], P('dp'), may hold values from -0.125 to 0.125
Outputs:
- scores: float32 [64, 64], P('dp')
Inputs may be any that keep to these rules, and one draw needn't show every extreme that they name: The candidates of many texts may all lie in the index rows of one device: in every draw at least half of the texts have all 64 of their candidates in the 512 index rows of one device, the same device for all of them.
All inputs are finite; a program needn't handle non-finite values. No bound on the sum of `lengths` on one device may be relied on, other than what follows from the above.
Results may differ from a plain program's by a relative error of at most 0.005.
Values may be sent and summed in bfloat16 or wider, within the bound.
A program may use at most 128 MiB of HBM per device.

v0:
```python
import jax
import jax.numpy as jnp
from jax import lax
from jax.sharding import PartitionSpec as P

HEAD = 64


def attend_text(bundle):
    queries, key_side, value_side, length = bundle
    slots = queries.shape[0]
    logits = jnp.einsum("qhd,khd->hqk", queries, key_side, preferred_element_type=jnp.float32)
    valid = jnp.arange(slots, dtype=jnp.int32) < length
    logits = jnp.where(valid[None, None, :], logits, jnp.float32(-1e30))
    probs = jax.nn.softmax(logits, axis=-1).astype(jnp.bfloat16)
    context = jnp.einsum("hqk,khd->qhd", probs, value_side, preferred_element_type=jnp.float32)
    return context.astype(jnp.bfloat16)


def per_device(
    hidden, lengths, order, candidates, norm_gain, w_query, w_key, w_value, w_out, index_rows
):
    texts, lmax, width = hidden.shape
    slots = texts * lmax
    features = w_query.shape[1]
    heads = features // HEAD
    flat = hidden.reshape(slots, width)
    values_f = flat.astype(jnp.float32)
    meansq = jnp.mean(values_f * values_f, axis=-1, keepdims=True)
    normed = (values_f * lax.rsqrt(meansq + 1e-06) * norm_gain).astype(jnp.bfloat16)
    full_query, full_key, full_value = (
        lax.all_gather(w_query, "dp", axis=0, tiled=True),
        lax.all_gather(w_key, "dp", axis=0, tiled=True),
        lax.all_gather(w_value, "dp", axis=0, tiled=True),
    )
    query_sum = jnp.dot(normed, full_query, preferred_element_type=jnp.float32)
    key_sum = jnp.dot(normed, full_key, preferred_element_type=jnp.float32)
    value_sum = jnp.dot(normed, full_value, preferred_element_type=jnp.float32)
    queries = query_sum.astype(jnp.bfloat16).reshape(texts, lmax, heads, HEAD)
    key_side = key_sum.astype(jnp.bfloat16).reshape(texts, lmax, heads, HEAD)
    value_side = value_sum.astype(jnp.bfloat16).reshape(texts, lmax, heads, HEAD)
    context = lax.map(attend_text, (queries, key_side, value_side, lengths)).reshape(
        slots, features
    )
    projected = jnp.dot(
        context, lax.all_gather(w_out, "dp", axis=0, tiled=True), preferred_element_type=jnp.float32
    )
    layer_out = (values_f + projected).reshape(texts, lmax, width)
    valid = jnp.arange(lmax, dtype=jnp.int32)[None, :] < lengths[:, None]
    pooled = (
        jnp.sum(jnp.where(valid[:, :, None], layer_out, jnp.float32(0.0)), axis=1)
        / lengths.astype(jnp.float32)[:, None]
    )
    unit = (pooled * lax.rsqrt(jnp.mean(pooled * pooled, axis=-1, keepdims=True) + 1e-06)).astype(
        jnp.bfloat16
    )
    order_all = lax.all_gather(order, "dp", axis=0, tiled=True)
    cand_proc = candidates[order_all]
    rows_dev = index_rows.shape[0]
    device = lax.axis_index("dp")
    local_scores = lax.dot_general(
        lax.all_gather(unit, "dp", axis=0, tiled=True),
        index_rows,
        (((1,), (1,)), ((), ())),
        preferred_element_type=jnp.float32,
    )
    owner = cand_proc // rows_dev
    within = cand_proc - owner * rows_dev
    picked = jnp.take_along_axis(local_scores, jnp.clip(within, 0, rows_dev - 1), axis=1)
    partial_value = jnp.where(owner == device, picked, jnp.float32(0.0))
    inverse = jnp.argsort(order_all)
    mine = lax.psum_scatter(partial_value, "dp", scatter_dimension=0, tiled=True)
    every_score = lax.all_gather(mine, "dp", axis=0, tiled=True)
    wanted_rows = lax.dynamic_slice_in_dim(inverse, device * texts, texts, 0)
    return every_score[wanted_rows]


def solution(mesh):
    return jax.shard_map(
        per_device,
        mesh=mesh,
        in_specs=(
            P("dp", None, None),
            P("dp"),
            P("dp"),
            P(),
            P(),
            P("dp", None),
            P("dp", None),
            P("dp", None),
            P("dp", None),
            P("dp", None),
        ),
        out_specs=P("dp", None),
        check_vma=False,
    )
```

profile of v0, /device:TPU:0, one launch (start us, length us, event | category | flops | bytes accessed | tf_op | source)
XLA Modules:
  0.0 438.8 jit_solution(18170291286663281299)
XLA Ops:
  6.6 0.7 all-gather.7.cloned.1.call-update
  7.3 0.7 all-gather.9.cloned.1.call-update
  8.1 0.7 all-gather.11.cloned.1.call-update
  8.8 0.5 all-gather.13.cloned.1.call-update
  9.3 1.3 iota_compare_fusion.1
  10.6 1.2 convert_element_type.43
  11.8 3.1 fusion.39
  15.0 0.2 dynamic-update-slice
  15.2 42.3 %all-reduce = s32[64]{0:T(128)S(1)} all-reduce(s32[64]{0:T(128)S(1)} %dynamic-update-slice), channel_id=1, replica_groups=mesh['dp'=32] {'dp'}, use_global_device_ids=true, to_apply=%add | all-reduce | flops 64 | bytes 512
  57.5 0.6 gather_fusion
  58.2 0.7 reshape.168
  58.8 2.1 sort.17
  60.9 0.1 compare_select_fusion.2
  61.0 0.6 pad_clamp_fusion
  61.6 5.2 %fusion.41 = bf16[1024,2048]{1,0:T(8,128)(2,1)} fusion(bf16[2,512,2048]{2,1,0:T(8,128)(2,1)} %param.12, f32[2048]{0:T(1024)S(1)} %copy-done.5, f32[1024]{0:T(1024)S(1)} %bitcast.102), kind=kLoop, calls=%fused_computation.36 | loop fusion | flops 8388608 | bytes 8400896 | tf_op jit(solution)/shard_map/convert_element_type | solution.py:30
  66.8 8.3 %all-gather.7.cloned.1.call-done = bf16[2048,1024]{1,0:T(8,128)(2,1)} async-done(((bf16[64,1024]{1,0:T(8,128)(2,1)}), bf16[2048,1024]{1,0:T(8,128)(2,1)}) %all-gather.7.cloned.1.call-update) | async-done | bytes 4194320 | tf_op jit(solution)/shard_map/all_gather | solution.py:34
  75.1 9.3 %convolution_convert_fusion.2 = bf16[1024,1024]{1,0:T(8,128)(2,1)} fusion(bf16[1024,2048]{1,0:T(8,128)(2,1)} %fusion.41, bf16[2048,1024]{1,0:T(8,128)(2,1)} %all-gather.7.cloned.1.call-done), kind=kOutput, calls=%fused_computation.40 | convolution fusion | flops 4296015872 | bytes 10485760 | tf_op jit(solution)/shard_map/dot_general | solution.py:38
  84.3 6.4 %reshape.182 = bf16[2,512,16,64]{3,2,1,0:T(8,128)(2,1)} reshape(bf16[1024,1024]{1,0:T(8,128)(2,1)} %convolution_convert_fusion.2) | data formatting | bytes 4194304 | tf_op jit(solution)/shard_map/reshape | solution.py:41
  90.8 5.5 %copy.27 = bf16[2,512,16,64]{1,3,2,0:T(8,128)(2,1)} copy(bf16[2,512,16,64]{3,2,1,0:T(8,128)(2,1)} %reshape.182) | data formatting | bytes 4194304 | tf_op jit(solution)/shard_map/while | solution.py:42
  96.2 42.3 %all-gather.9.cloned.1.call-done = bf16[2048,1024]{1,0:T(8,128)(2,1)} async-done(((bf16[64,1024]{1,0:T(8,128)(2,1)}), bf16[2048,1024]{1,0:T(8,128)(2,1)}) %all-gather.9.cloned.1.call-update) | async-done | bytes 4194320 | tf_op jit(solution)/shard_map/all_gather | solution.py:32
  138.5 9.3 %convolution_convert_fusion.1 = bf16[1024,1024]{1,0:T(8,128)(2,1)} fusion(bf16[1024,2048]{1,0:T(8,128)(2,1)} %fusion.41, bf16[2048,1024]{1,0:T(8,128)(2,1)} %all-gather.9.cloned.1.call-done), kind=kOutput, calls=%fused_computation.39 | convolution fusion | flops 4296015872 | bytes 10485760 | tf_op jit(solution)/shard_map/dot_general | solution.py:36
  147.8 6.4 %reshape.183 = bf16[2,512,16,64]{3,2,1,0:T(8,128)(2,1)} reshape(bf16[1024,1024]{1,0:T(8,128)(2,1)} %convolution_convert_fusion.1) | data formatting | bytes 4194304 | tf_op jit(solution)/shard_map/reshape | solution.py:39
  154.2 5.4 %copy.28 = bf16[2,512,16,64]{1,3,2,0:T(8,128)(2,1)} copy(bf16[2,512,16,64]{3,2,1,0:T(8,128)(2,1)} %reshape.183) | data formatting | bytes 4194304 | tf_op jit(solution)/shard_map/while | solution.py:42
  159.7 42.4 %all-gather.11.cloned.1.call-done = bf16[2048,1024]{1,0:T(8,128)(2,1)} async-done(((bf16[64,1024]{1,0:T(8,128)(2,1)}), bf16[2048,1024]{1,0:T(8,128)(2,1)}) %all-gather.11.cloned.1.call-update) | async-done | bytes 4194320 | tf_op jit(solution)/shard_map/all_gather | solution.py:33
  202.0 9.3 %convolution_convert_fusion = bf16[1024,1024]{1,0:T(8,128)(2,1)} fusion(bf16[1024,2048]{1,0:T(8,128)(2,1)} %fusion.41, bf16[2048,1024]{1,0:T(8,128)(2,1)} %all-gather.11.cloned.1.call-done), kind=kOutput, calls=%fused_computation.38 | convolution fusion | flops 4296015872 | bytes 10485760 | tf_op jit(solution)/shard_map/dot_general | solution.py:37
  211.3 6.4 %reshape.184 = bf16[2,512,16,64]{3,2,1,0:T(8,128)(2,1)} reshape(bf16[1024,1024]{1,0:T(8,128)(2,1)} %convolution_convert_fusion) | data formatting | bytes 4194304 | tf_op jit(solution)/shard_map/reshape | solution.py:40
  217.7 5.5 %copy.29 = bf16[2,512,16,64]{1,3,2,0:T(8,128)(2,1)} copy(bf16[2,512,16,64]{3,2,1,0:T(8,128)(2,1)} %reshape.184) | data formatting | bytes 4194304 | tf_op jit(solution)/shard_map/while | solution.py:42
  223.2 41.8 %while.10 = (s32[]{:T(128)}, bf16[2,512,16,64]{1,3,2,0:T(8,128)(2,1)}, bf16[2,512,16,64]{1,3,2,0:T(8,128)(2,1)}, s32[2]{0:T(128)S(1)}, bf16[2,512,16,64]{1,3,2,0...) while((s32[]{:T(128)}, bf16[2,512,16,64]{1,3,2,0:T(8,128)(2,1)}, ...), condition=%wide.region_4.5_spmd, body=%wide.region_1.4_spmd.sunk | while | flops 1095238656 | bytes 37817436 | solution.py:42
  223.2 0.7 dynamic_slice.62
  223.8 0.7 iota_compare_fusion.3
  224.5 10.8 %fusion.82 = (f32[16,512]{1,0:T(8,128)S(1)}, f32[16,512,512]{1,2,0:T(8,128)}) fusion(pred[512]{0:T(512)(128)(4,1)S(1)} %iota_compare_fusion.3, bf16[2,512,16,64]{1,3,2,0:T(8,128)(2,1)} %get-tuple-element.134, s32[]{:T(128)} %get-tuple-element.122, bf16[2,512,16,64]{1,3,2,0:T(8,128)(2,1)} %get-tuple-element.133), kind=kOutput, calls=%fused_computation.78.clone.1 | convolution fusion | flops 549454336 | bytes 18908672 | tf_op jit(solution)/shard_map/while/body/eval_jaxpr/sub | solution.py:15
  235.3 8.7 %fusion.83 = bf16[2,512,16,64]{1,3,2,0:T(8,128)(2,1)} fusion(bf16[2,512,16,64]{1,3,2,0:T(8,128)(2,1)} %get-tuple-element.123, s32[]{:T(128)} %get-tuple-element.122, f32[16,512,512]{1,2,0:T(8,128)} %get-tuple-element.113, f32[16,512]{1,0:T(8,128)S(1)} %get-tuple-element.114, bf16[2,512,16,64]{1,3,2,0:T(8,128)(2,1)} %get-tuple-element.131), kind=kOutput, calls=%fused_computation.14.clone.1 | convolution fusion | flops 545783808 | bytes 18908160 | tf_op jit(solution)/shard_map/while/body/eval_jaxpr/hqk,khd->qhd/dot_general | solution.py:16
  244.0 0.7 dynamic_slice.62
  244.7 0.7 iota_compare_fusion.3
  245.4 10.8 %fusion.82 = (f32[16,512]{1,0:T(8,128)S(1)}, f32[16,512,512]{1,2,0:T(8,128)}) fusion(pred[512]{0:T(512)(128)(4,1)S(1)} %iota_compare_fusion.3, bf16[2,512,16,64]{1,3,2,0:T(8,128)(2,1)} %get-tuple-element.134, s32[]{:T(128)} %get-tuple-element.122, bf16[2,512,16,64]{1,3,2,0:T(8,128)(2,1)} %get-tuple-element.133), kind=kOutput, calls=%fused_computation.78.clone.1 | convolution fusion | flops 549454336 | bytes 18908672 | tf_op jit(solution)/shard_map/while/body/eval_jaxpr/sub | solution.py:15
  256.1 8.8 %fusion.83 = bf16[2,512,16,64]{1,3,2,0:T(8,128)(2,1)} fusion(bf16[2,512,16,64]{1,3,2,0:T(8,128)(2,1)} %get-tuple-element.123, s32[]{:T(128)} %get-tuple-element.122, f32[16,512,512]{1,2,0:T(8,128)} %get-tuple-element.113, f32[16,512]{1,0:T(8,128)S(1)} %get-tuple-element.114, bf16[2,512,16,64]{1,3,2,0:T(8,128)(2,1)} %get-tuple-element.131), kind=kOutput, calls=%fused_computation.14.clone.1 | convolution fusion | flops 545783808 | bytes 18908160 | tf_op jit(solution)/shard_map/while/body/eval_jaxpr/hqk,khd->qhd/dot_general | solution.py:16
  265.0 3.8 copy.30
  268.7 1.9 copy.39
  270.7 9.2 %select_reduce_fusion.1 = f32[2,2048]{1,0:T(2,128)S(1)} fusion(pred[2,512]{1,0:T(4,128)(4,1)S(1)} %copy-done.6, bf16[1024,1024]{0,1:T(8,128)(2,1)} %bitcast.100, bf16[1024,2048]{1,0:T(8,128)(2,1)} %all-gather.13.cloned.1.call-done, bf16[2,512,2048]{2,1,0:T(8,128)(2,1)} %param.12), kind=kOutput, calls=%fused_computation.37 | convolution fusion | flops 4303351808 | bytes 10503168 | tf_op jit(solution)/shard_map/dot_general | solution.py:45
  279.9 0.2 multiply_reduce_fusion
  280.1 0.1 fusion.53
  280.2 39.8 %all-gather = bf16[32,2,2048]{2,1,0:T(2,128)(2,1)S(1)} all-gather(bf16[1,2,2048]{2,1,0:T(2,128)(2,1)S(1)} %fusion.53), channel_id=1, replica_groups=mesh['dp'=32] {'dp'}, dimensions={0}, use_global_device_ids=true | all-gather | bytes 270336 | tf_op jit(solution)/shard_map/all_gather | solution.py:62
  320.0 0.1 reshape.179
  320.1 0.8 fusion.63
  320.9 32.8 %gather_fusion.2 = f32[4096]{0:T(1024)S(1)} fusion(f32[64,512]{1,0:T(8,128)S(1)} %fusion.63, s32[4096]{0:T(1024)S(1)} %copy-done.1), kind=kCustom, calls=%fused_computation.2 | custom fusion | bytes 65536 | tf_op jit(solution)/shard_map/jit(take_along_axis)/gather | solution.py:69
  353.8 37.0 %all-reduce.1 = f32[64,64]{1,0:T(8,128)S(1)} all-reduce(f32[64,64]{1,0:T(8,128)S(1)} %select_select_fusion), channel_id=2, replica_groups=mesh['dp'=32] {'dp'}, use_global_device_ids=true, to_apply=%region_7.8.clone | all-reduce | flops 4096 | bytes 32768
  390.8 40.2 %all-gather.1 = f32[32,2,64]{2,1,0:T(2,128)S(1)} all-gather(f32[1,2,64]{2,1,0:T(2,128)S(1)} %dynamic-slice_bitcast_fusion), channel_id=1, replica_groups=mesh['dp'=32] {'dp'}, dimensions={0}, use_global_device_ids=true | all-gather | bytes 16896 | tf_op jit(solution)/shard_map/all_gather | solution.py:73
  431.0 1.2 gather_fusion.1
  (37 shorter events, 0.4 us)
Async XLA Ops:
  6.5 313.5 %copy-start = (bf16[512,2048]{1,0:T(8,128)(2,1)S(1)}, bf16[512,2048]{1,0:T(8,128)(2,1)}, u32[]{:S(2)}) copy-start(bf16[512,2048]{1,0:T(8,128)(2,1)} %param.21) | copy-start | bytes 6291460
  6.5 8.4 %copy-start.9 = (s32[2]{0:T(128)S(1)}, s32[2]{0:T(128)}, u32[]{:S(2)}) copy-start(s32[2]{0:T(128)} %param.14) | copy-start | bytes 28
  6.5 51.0 %copy-start.2 = (s32[64,64]{1,0:T(8,128)S(1)}, s32[64,64]{1,0:T(8,128)}, u32[]{:S(2)}) copy-start(s32[64,64]{1,0:T(8,128)} %param.15) | copy-start | bytes 49156
  6.5 55.1 %copy-start.5 = (f32[2048]{0:T(1024)S(1)}, f32[2048]{0:T(1024)}, u32[]{:S(2)}) copy-start(f32[2048]{0:T(1024)} %param.16) | copy-start | bytes 24580
  6.5 68.5 %all-gather.7.cloned.1.call-start = ((), (), s32[]{:S(2)}) async-start(), calls=%async_computation | async-start | bytes 4325376 | tf_op jit(solution)/shard_map/all_gather | solution.py:34
  7.3 131.3 %all-gather.9.cloned.1.call-start = ((), (), s32[]{:S(2)}) async-start(), calls=%async_computation.1 | async-start | bytes 4325376 | tf_op jit(solution)/shard_map/all_gather | solution.py:32
  8.0 194.0 %all-gather.11.cloned.1.call-start = ((), (), s32[]{:S(2)}) async-start(), calls=%async_computation.2 | async-start | bytes 4325376 | tf_op jit(solution)/shard_map/all_gather | solution.py:33
  8.8 261.9 %all-gather.13.cloned.1.call-start = ((), (), s32[]{:S(2)}) async-start(), calls=%async_computation.3 | async-start | bytes 4325376 | tf_op jit(solution)/shard_map/all_gather | solution.py:46
  58.1 8.7 %copy-start.3 = (s32[64,64]{1,0:T(8,128)}, s32[64,64]{1,0:T(8,128)S(1)}, u32[]{:S(2)}) copy-start(s32[64,64]{1,0:T(8,128)S(1)} %gather_fusion) | copy-start | bytes 49156
  217.7 5.5 %copy-start.8 = (s32[2]{0:T(128)S(1)}, s32[2]{0:T(128)}, u32[]{:S(2)}) copy-start(s32[2]{0:T(128)} %param.13) | copy-start | bytes 28
  265.0 5.7 %copy-start.6 = (pred[2,512]{1,0:T(4,128)(4,1)S(1)}, pred[2,512]{1,0:T(4,128)(4,1)}, u32[]{:S(2)}) copy-start(pred[2,512]{1,0:T(4,128)(4,1)} %iota_compare_fusion.1) | copy-start | bytes 3076
  270.7 9.2 %copy-start.7 = (f32[2]{0:T(128)S(1)}, f32[2]{0:T(128)}, u32[]{:S(2)}) copy-start(f32[2]{0:T(128)} %convert_element_type.43) | copy-start | bytes 28
  279.9 40.9 %copy-start.1 = (s32[4096]{0:T(1024)S(1)}, s32[4096]{0:T(1024)}, u32[]{:S(2)}) copy-start(s32[4096]{0:T(1024)} %reshape.168) | copy-start | bytes 49156
  320.9 32.9 %copy-start.4 = (s32[64,64]{1,0:T(8,128)S(1)}, s32[64,64]{1,0:T(8,128)}, u32[]{:S(2)}) copy-start(s32[64,64]{1,0:T(8,128)} %copy-done.3) | copy-start | bytes 49156
Sparse Core Ops, SparseCore 0:
  10.2 64.7 all-gather.6
  77.9 60.5 all-gather.8
  141.4 60.5 all-gather.10
  204.7 60.5 all-gather.12
where the time goes:
time: 440 us; the launch traced here: 439 us
  blocking collectives  159 us (36%)
  waiting for transfers between devices  95.5 us (22%)
  local copies, waits for them, and re-layouts  78.3 us (18%)
  matrix products  77 us (18%)
  other arithmetic  15.3 us (3%)
  between operations  13.3 us (3%)
    unnamed x2, blocking collectives  79.3 us
    all_gather x1, waiting for transfers between devices, per_device(): lax.all_gather(w_key, 'dp', axis=0, tiled=True)  42.4 us
    all_gather x1, waiting for transfers between devices, per_device(): lax.all_gather(w_query, 'dp', axis=0, tiled=True)  42.3 us
    all_gather x1, blocking collectives, per_device(): every_score = lax.all_gather(mine, 'dp', axis=0, tiled=True)  40.2 us
    all_gather x1, blocking collectives, per_device(): lax.all_gather(unit, 'dp', axis=0, tiled=True)  39.8 us
    gather x3, local copies, waits for them, and re-layouts, per_device(): jnp.take_along_axis(local_scores, jnp.clip(within, 0, rows_dev - 1), axis=1)  33.5 us
    sub x2, matrix products, attend_text(): probs = jax.nn.softmax(logits, axis=-1).astype(jnp.bfloat16)  21.5 us
    while x4, local copies, waits for them, and re-layouts, per_device(): lax.map(attend_text, (queries, key_side, value_side, lengths))  20.1 us
  transfers between devices with their start and end apart: 4, of which 3 were waited for; matrix products, arithmetic and copies ran while one was open for 29% of the time, Pallas kernels for 0%

commit v1 on v0

v1 whole, which is shorter than its diff:
```python
import functools

import jax
import jax.numpy as jnp
from jax import lax
from jax.experimental import pallas as pl
from jax.experimental.pallas import tpu as pltpu
from jax.sharding import PartitionSpec as P

HEAD = 64
MESH = pl.DeviceIdType.MESH
F32 = jnp.float32
BF16 = jnp.bfloat16


def grid_of(count):
    chips = count // 2
    side = 4 if chips >= 64 else 2
    return chips // (side * side), side, side


def split_rows(value):
    high = value.astype(BF16)
    low = (value - high.astype(F32)).astype(BF16)
    return jnp.concatenate([high, low], axis=0)


def encode_kernel(
    count, gather_out, lengths_ref, hidden_hbm, gain_ref, wq_hbm, wk_hbm, wv_hbm, wo_hbm,
    unit_ref, hidden_ref, normed_ref, gq, gk, gv, go, q_ref, k_ref, psum_ref, send, recv, local,
):
    planes, rows, cols = grid_of(count)
    me = lax.axis_index("dp")
    core = lax.rem(me, 2)
    b = lax.rem(me // 2, cols)
    a = lax.rem(me // (2 * cols), rows)
    z = me // (2 * cols * rows)
    texts = lengths_ref.shape[0]
    slots, width = hidden_ref.shape
    lmax = slots // texts
    heads = q_ref.shape[1] // HEAD

    def device(zz, aa, bb, cc):
        return ((zz * rows + aa) * cols + bb) * 2 + cc

    def others(size, own):
        return [lax.rem(own + step, size) for step in range(1, size)]

    z_line = [device(o, a, b, core) for o in others(planes, z)]
    a_line = [device(z, o, b, core) for o in others(rows, a)]
    b_line = [device(z, a, o, core) for o in others(cols, b)]
    twin = device(z, a, b, 1 - core)

    hidden_copy = pltpu.make_async_copy(hidden_hbm, hidden_ref, local.at[0])
    hidden_copy.start()

    pieces = []
    for source, held in ((wq_hbm, gq), (wk_hbm, gk)):
        half = source.shape[1] // 2
        pieces += [(source, held, 0, half), (source, held, half, half)]
    pieces = [pieces[0], pieces[2], pieces[1], pieces[3]]
    for source, held in ((wv_hbm, gv), (wo_hbm, go)):
        if source is wo_hbm and not gather_out:
            continue
        half = source.shape[1] // 2
        pieces += [(source, held, 0, half), (source, held, half, half)]

    local_copies = []
    for i, (source, held, start, size) in enumerate(pieces):
        copy = pltpu.make_async_copy(
            source.at[:, pl.ds(start, size)],
            held.at[z, a, b, core, :, pl.ds(start, size)],
            local.at[1 + i],
        )
        copy.start()
        local_copies.append(copy)
    if not gather_out:
        out_copy = pltpu.make_async_copy(wo_hbm, go, local.at[1 + len(pieces)])
        out_copy.start()

    barrier = pltpu.get_barrier_semaphore()
    partners = z_line + a_line + b_line + [twin]
    for other in partners:
        pl.semaphore_signal(barrier, inc=1, device_id=(other,), device_id_type=MESH)
    pl.semaphore_wait(barrier, len(partners))

    stages = []
    for i, (source, held, start, size) in enumerate(pieces):
        slot = 0
        half = size // 2
        first, second = pl.ds(start, half), pl.ds(start + half, half)
        whole = pl.ds(start, size)
        plan = ([], [], [], [])

        def add(stage, src, dst, target):
            nonlocal slot
            plan[stage].append(
                pltpu.make_async_remote_copy(
                    src_ref=src, dst_ref=dst, send_sem=send.at[i, slot],
                    recv_sem=recv.at[i, slot], device_id=(target,), device_id_type=MESH,
                )
            )
            slot += 1

        for target in z_line:
            add(0, source.at[:, whole], held.at[z, a, b, core, :, whole], target)
        for target in b_line:
            part = held.at[:, a, b, core, :, first]
            add(1, part, part, target)
        for target in a_line:
            part = held.at[:, a, b, core, :, second]
            add(1, part, part, target)
        for target in a_line:
            part = held.at[:, a, :, core, :, first]
            add(2, part, part, target)
        for target in b_line:
            part = held.at[:, :, b, core, :, second]
            add(2, part, part, target)
        part = held.at[:, :, :, core, :, whole]
        add(3, part, part, twin)
        stages.append(plan)

    def begin(piece, stage):
        if 0 <= piece < len(pieces):
            if stage == 1:
                local_copies[piece].wait()
            for copy in stages[piece][stage]:
                copy.start()

    def finish(piece, stage):
        if 0 <= piece < len(pieces):
            for copy in stages[piece][stage]:
                copy.wait()

    def advance(step):
        finish(step, 0)
        begin(step, 1)
        begin(step + 2, 0)
        finish(step - 1, 1)
        begin(step - 1, 2)
        finish(step - 2, 2)
        begin(step - 2, 3)
        finish(step - 3, 3)

    def norm_rows():
        tile = 128

        @pl.loop(0, slots // tile)
        def _(i):
            at = pl.ds(pl.multiple_of(i * tile, tile), tile)
            x = hidden_ref[at, :].astype(F32)
            mean = jnp.mean(x * x, axis=-1, keepdims=True)
            normed_ref[at, :] = (x * lax.rsqrt(mean + 1e-06) * gain_ref[...]).astype(BF16)

    def project(held, out, start, size):
        tile = 256

        @pl.loop(0, slots // tile)
        def _(i):
            at = pl.ds(pl.multiple_of(i * tile, tile), tile)
            for c in range(start, start + size, 256):
                w = held[:, :, :, :, :, c:c + 256].reshape(width, 256)
                out[at, c:c + 256] = jnp.dot(
                    normed_ref[at, :], w, preferred_element_type=F32
                ).astype(BF16)

    def attend(head_start, head_stop):
        lane = lax.broadcasted_iota(jnp.int32, (1, 2 * HEAD), 1)
        key_slot = lax.broadcasted_iota(jnp.int32, (1, lmax), 1)
        query_slot = lax.broadcasted_iota(jnp.int32, (lmax, 1), 0)
        for t in range(texts):
            length = lengths_ref[t]
            key_valid = key_slot < length
            query_valid = query_slot < length

            @pl.loop(head_start // 2, head_stop // 2)
            def _(pair):
                at = pl.ds(pl.multiple_of(pair * 2 * HEAD, 2 * HEAD), 2 * HEAD)
                q = q_ref[t * lmax:(t + 1) * lmax, at]
                k = k_ref[t * lmax:(t + 1) * lmax, at]
                sums = []
                for side in range(2):
                    q_one = jnp.where((lane // HEAD) == side, q, jnp.zeros_like(q))
                    logits = lax.dot_general(
                        q_one, k, (((1,), (1,)), ((), ())), preferred_element_type=F32
                    )
                    logits = jnp.where(key_valid, logits, F32(-1e30))
                    top = jnp.max(logits, axis=1, keepdims=True)
                    e = jnp.exp(logits - top)
                    weight = jnp.where(
                        query_valid, 1.0 / jnp.sum(e, axis=1, keepdims=True), F32(0.0)
                    )
                    sums.append(jnp.sum(e * weight, axis=0, keepdims=True))
                psum_ref[t, pl.ds(pair, 1), 0:lmax] = sums[0]
                psum_ref[t, pl.ds(pair, 1), lmax:2 * lmax] = sums[1]

    begin(0, 0)
    begin(1, 0)
    hidden_copy.wait()
    norm_rows()
    half_width = q_ref.shape[1] // 2
    quarter = heads // 4
    combined = []

    def combine():
        for t in range(texts):
            both = jnp.concatenate(
                [psum_ref[t, :, 0:lmax], psum_ref[t, :, lmax:2 * lmax]], axis=0
            )
            part = jnp.dot(
                split_rows(both), normed_ref[t * lmax:(t + 1) * lmax, :],
                preferred_element_type=F32,
            )
            combined.append(part[0:heads] + part[heads:2 * heads])

    for step in range(len(pieces) + 3):
        advance(step)
        if step == 3:
            project(gq, q_ref, 0, half_width)
        elif step == 4:
            project(gk, k_ref, 0, half_width)
            attend(0, quarter)
        elif step == 5:
            project(gq, q_ref, half_width, half_width)
            attend(quarter, 2 * quarter)
        elif step == 6:
            project(gk, k_ref, half_width, half_width)
            attend(2 * quarter, 3 * quarter)
        elif step == 7:
            attend(3 * quarter, heads)
            combine()
    if not gather_out:
        out_copy.wait()

    stacked = split_rows(jnp.concatenate(combined, axis=0))
    features = gv.shape[-1]
    lane = lax.broadcasted_iota(jnp.int32, (heads, features), 1)
    row = lax.broadcasted_iota(jnp.int32, (heads, features), 0)
    head = jnp.where(row < heads // 2, 2 * row, 2 * (row - heads // 2) + 1)
    pieces_v = []
    for c in range(0, features, 256):
        w = gv[:, :, :, :, :, c:c + 256].reshape(width, 256)
        pieces_v.append(jnp.dot(stacked, w, preferred_element_type=F32))
    spread = jnp.concatenate(pieces_v, axis=1)
    spread = spread[0:texts * heads] + spread[texts * heads:2 * texts * heads]
    contexts = [
        jnp.sum(
            jnp.where(lane // HEAD == head, spread[t * heads:(t + 1) * heads], F32(0.0)),
            axis=0, keepdims=True,
        )
        for t in range(texts)
    ]
    key_slot = lax.broadcasted_iota(jnp.int32, (16, lmax), 1)
    for t in range(texts):
        context = jnp.broadcast_to(contexts[t], (8, features))
        both = split_rows(context)
        valid = jnp.where(key_slot < lengths_ref[t], 1.0, 0.0).astype(BF16)
        total = jnp.dot(
            valid, hidden_ref[t * lmax:(t + 1) * lmax, :], preferred_element_type=F32
        )[0:8]
        outs = []
        for c in range(0, width, 512):
            if gather_out:
                w = go[:, :, :, :, :, c:c + 512].reshape(features, 512)
            else:
                w = go[:, c:c + 512]
            piece = jnp.dot(both, w, preferred_element_type=F32)
            outs.append(piece[0:8] + piece[8:16])
        pooled = (total + jnp.concatenate(outs, axis=1)) / lengths_ref[t].astype(F32)
        mean = jnp.mean(pooled * pooled, axis=-1, keepdims=True)
        unit_ref[t:t + 1, :] = (pooled * lax.rsqrt(mean + 1e-06))[0:1]


def encode(count, lengths, hidden, gain, w_query, w_key, w_value, w_out):
    planes, rows, cols = grid_of(count)
    texts, lmax, width = hidden.shape
    slots, features = texts * lmax, w_query.shape[1]
    gather_out = w_out.shape[0] % 16 == 0
    if not gather_out:
        w_out = lax.all_gather(w_out, "dp", axis=0, tiled=True)
    lead = (planes, rows, cols, 2)
    held = pltpu.VMEM(lead + w_query.shape, BF16)
    copies = planes - 1 + 2 * (rows - 1 + cols - 1) + 1
    return pl.pallas_call(
        functools.partial(encode_kernel, count, gather_out),
        out_shape=jax.ShapeDtypeStruct((texts, width), F32),
        in_specs=[
            pl.BlockSpec(memory_space=pltpu.SMEM),
            pl.BlockSpec(memory_space=pl.ANY),
            pl.BlockSpec(memory_space=pltpu.VMEM),
            pl.BlockSpec(memory_space=pl.ANY),
            pl.BlockSpec(memory_space=pl.ANY),
            pl.BlockSpec(memory_space=pl.ANY),
            pl.BlockSpec(memory_space=pl.ANY),
        ],
        out_specs=pl.BlockSpec(memory_space=pltpu.VMEM),
        scratch_shapes=[
            pltpu.VMEM((slots, width), BF16),
            pltpu.VMEM((slots, width), BF16),
            held, held, held,
            pltpu.VMEM((lead if gather_out else ()) + w_out.shape, BF16),
            pltpu.VMEM((slots, features), BF16),
            pltpu.VMEM((slots, features), BF16),
            pltpu.VMEM((texts, features // HEAD // 2, 2 * lmax), F32),
            pltpu.SemaphoreType.DMA((8, copies)),
            pltpu.SemaphoreType.DMA((8, copies)),
            pltpu.SemaphoreType.DMA((10,)),
        ],
        compiler_params=pltpu.CompilerParams(
            collective_id=0, has_side_effects=True, vmem_limit_bytes=56 * 1024 * 1024
        ),
        cost_estimate=pl.CostEstimate(
            flops=10 ** 10, bytes_accessed=24 * 2 ** 20, transcendentals=2 ** 23
        ),
    )(lengths, hidden.reshape(slots, width), gain.reshape(1, width), w_query, w_key, w_value, w_out)


def score_kernel(
    count, note_ref, index_ref, cand_ref, out_ref, got, mine, back, send, recv, send2, recv2
):
    me = lax.axis_index("dp")
    texts = out_ref.shape[0]
    total = count * texts
    rows_dev, width = index_ref.shape
    wide = width // 8

    def to(step):
        return lax.rem(me + step, count)

    def source(step):
        return lax.rem(me + count - step, count)

    barrier = pltpu.get_barrier_semaphore()

    @pl.loop(1, count)
    def _(step):
        pl.semaphore_signal(barrier, inc=1, device_id=(to(step),), device_id_type=MESH)

    pl.semaphore_wait(barrier, count - 1)

    def note_copy(step, place, target):
        return pltpu.make_async_remote_copy(
            src_ref=note_ref, dst_ref=got.at[place], send_sem=send.at[step],
            recv_sem=recv.at[step], device_id=(target,), device_id_type=MESH,
        )

    @pl.loop(1, count)
    def _(step):
        note_copy(step, me, to(step)).start()

    got[me] = note_ref[...]

    @pl.loop(1, count)
    def _(step):
        note_copy(step, source(step), to(step)).wait_recv()

    flat = got[...].reshape(count * texts * 8, wide + 128)
    data = flat[:, 0:wide]
    numbers = flat[:, wide:wide + 128].astype(F32).T[0:1, :].astype(jnp.int32)
    span = count * texts * 8
    lane = lax.broadcasted_iota(jnp.int32, (total, span), 1)
    row = lax.broadcasted_iota(jnp.int32, (total, span), 0)
    same = numbers == row
    scores = jnp.zeros((total, rows_dev), F32)
    for k in range(8):
        pick = jnp.where(same & (lax.rem(lane, 8) == k), 1.0, 0.0).astype(BF16)
        unit = jnp.dot(pick, data, preferred_element_type=F32).astype(BF16)
        scores += lax.dot_general(
            unit, index_ref[:, k * wide:(k + 1) * wide], (((1,), (1,)), ((), ())),
            preferred_element_type=F32,
        )
    within = cand_ref[...] - me * rows_dev
    slot = lax.broadcasted_iota(jnp.int32, (1, 1, rows_dev), 2)
    for r in range(0, total, 8):
        hit = within[r:r + 8][:, :, None] == slot
        part = jnp.sum(jnp.where(hit, scores[r:r + 8][:, None, :], F32(0.0)), axis=2)
        for j in range(0, 8, texts):
            mine[(r + j) // texts] = part[j:j + texts, :]

    def back_copy(step, target, place):
        return pltpu.make_async_remote_copy(
            src_ref=mine.at[target], dst_ref=back.at[place], send_sem=send2.at[step],
            recv_sem=recv2.at[step], device_id=(target,), device_id_type=MESH,
        )

    @pl.loop(1, count)
    def _(step):
        back_copy(step, to(step), me).start()

    back[me] = mine[me]

    @pl.loop(1, count)
    def _(step):
        back_copy(step, to(step), source(step)).wait_recv()

    out_ref[...] = jnp.sum(back[...], axis=0)

    @pl.loop(1, count)
    def _(step):
        note_copy(step, source(step), to(step)).wait_send()
        back_copy(step, to(step), source(step)).wait_send()


def score(count, note, index_rows, candidates, texts):
    cand = candidates.shape[1]
    return pl.pallas_call(
        functools.partial(score_kernel, count),
        out_shape=jax.ShapeDtypeStruct((texts, cand), F32),
        in_specs=[pl.BlockSpec(memory_space=pltpu.VMEM)] * 3,
        out_specs=pl.BlockSpec(memory_space=pltpu.VMEM),
        scratch_shapes=[
            pltpu.VMEM((count,) + note.shape, BF16),
            pltpu.VMEM((count, texts, cand), F32),
            pltpu.VMEM((count, texts, cand), F32),
            pltpu.SemaphoreType.DMA((count,)),
            pltpu.SemaphoreType.DMA((count,)),
            pltpu.SemaphoreType.DMA((count,)),
            pltpu.SemaphoreType.DMA((count,)),
        ],
        compiler_params=pltpu.CompilerParams(
            collective_id=1, has_side_effects=True, vmem_limit_bytes=48 * 1024 * 1024
        ),
        cost_estimate=pl.CostEstimate(
            flops=3 * 10 ** 8, bytes_accessed=4 * 2 ** 20, transcendentals=0
        ),
    )(note, index_rows, candidates)


def solution(mesh):
    count = mesh.shape["dp"]

    def per_device(
        hidden, lengths, order, candidates, norm_gain, w_query, w_key, w_value, w_out, index_rows
    ):
        texts, _, width = hidden.shape
        unit = encode(count, lengths, hidden, norm_gain, w_query, w_key, w_value, w_out)
        wide = width // 8
        number = jnp.broadcast_to(order.astype(BF16)[:, None, None], (texts, 8, 128))
        note = jnp.concatenate([unit.reshape(texts, 8, wide).astype(BF16), number], axis=2)
        note = note.reshape(texts * 8, wide + 128)
        return score(count, note, index_rows, candidates, texts)

    return jax.shard_map(
        per_device,
        mesh=mesh,
        in_specs=(
            P("dp", None, None),
            P("dp"),
            P("dp"),
            P(),
            P(),
            P("dp", None),
            P("dp", None),
            P("dp", None),
            P("dp", None),
            P("dp", None),
        ),
        out_specs=P("dp", None),
        check_vma=False,
    )
```

time: 440 us -> 121 us (0.28)
  blocking collectives: 159 us -> 0 us
  Pallas kernels: 0 us -> 119 us
  waiting for transfers between devices: 95.5 us -> 0 us
  local copies, waits for them, and re-layouts: 78.3 us -> 0.83 us
  matrix products: 77 us -> 0 us
  other arithmetic: 15.3 us -> 0.74 us
  between operations: 13.3 us -> 0.03 us
    pallas_call x0 -> x2, Pallas kernels: none -> 119 us  [the longest x1 90.4 us: encode(): pl.pallas_call(functools.partial(encode_kernel, count, gather_out), out_s...]
    all_gather x4 -> x0, waiting for transfers between devices: 92.9 us -> none  [the longest x1 42.4 us: per_device(): lax.all_gather(w_key, 'dp', axis=0, tiled=True)]
    all_gather x2 -> x0, blocking collectives: 80 us -> none  [the longest x1 40.2 us: per_device(): every_score = lax.all_gather(mine, 'dp', axis=0, tiled=True)]
    unnamed x2 -> x0, blocking collectives: 79.3 us -> none
    dot_general x7 -> x0, matrix products: 55.4 us -> none  [the longest x2 17.6 us: attend_text(): jnp.einsum('hqk,khd->qhd', probs, value_side, preferred_element_type=jnp....]
    gather x5 -> x0, local copies, waits for them, and re-layouts: 35.3 us -> none  [the longest x3 33.5 us: per_device(): jnp.take_along_axis(local_scores, jnp.clip(within, 0, rows_dev - 1), axis=1)]
    sub x2 -> x0, matrix products: 21.5 us -> none  [attend_text(): probs = jax.nn.softmax(logits, axis=-1).astype(jnp.bfloat16)]
    while x4 -> x0, local copies, waits for them, and re-layouts: 20.1 us -> none  [per_device(): lax.map(attend_text, (queries, key_side, value_side, lengths))]
  transfers between devices with their start and end apart: 4 -> 0, of which waited for: 3 -> 0; matrix products, arithmetic and copies ran while one was open for 29% -> 0% of each run, Pallas kernels for 0% -> 0%
where the time goes in v1:
time: 121 us
  Pallas kernels  119 us (98%)
    pallas_call x1, Pallas kernels, encode(): pl.pallas_call(functools.partial(encode_kernel, count, gather_out), out_s...  90.4 us
    pallas_call x1, Pallas kernels, score(): pl.pallas_call(functools.partial(score_kernel, count), out_shape=jax.Shap...  28.8 us

profile of v1, /device:TPU:0, one launch (start us, length us, event | category | flops | bytes accessed | tf_op | source)
XLA Modules:
  0.0 120.8 jit_solution(14865238124585912815)
XLA Ops:
  0.0 0.0 copy-start.2
  0.0 0.0 copy-start
  0.0 0.0 copy-start.1
  0.0 90.4 %shard_map.100 = f32[2,2048]{1,0:T(2,128)} custom-call(s32[2]{0:T(128)} %lengths_ref.1, bf16[1024,2048]{1,0:T(8,128)(2,1)} %bitcast.2, f32[1,2048]{1,0:T(1,128)} %bitcast.3, bf16[64,1024]{1,0:T(8,128)(2,1)} %wq_hbm.1, bf16[64,1024]{1,0:T(8,128)(2,1)} %wk_hbm.1, bf16[64,1024]{1,0:T(8,128)(2,1)} %wv_hbm.1, bf16[32,2048]{1,0:T(8,128)(2,1)} %wo_hbm.1), custom_call_target="tpu_custom_call" | custom-call | flops 10000000000 | bytes 25165824 | tf_op jit(solution)/shard_map/pallas_call | solution.py:284
  90.4 0.7 convert_element_type.10
  91.2 0.0 copy-done.2
  91.2 0.1 broadcast_in_dim.10
  91.3 0.1 broadcast_in_dim.11
  91.3 0.1 broadcast_in_dim.12
  91.4 0.0 copy-done
  91.4 0.0 copy-done.1
  91.4 28.8 %shard_map.101 = f32[2,64]{1,0:T(2,128)S(1)} custom-call(bf16[16,384]{1,0:T(8,128)(2,1)S(1)} %pad_maximum_fusion.note_ref, bf16[512,2048]{1,0:T(8,128)(2,1)S(1)} %copy-done, s32[64,64]{1,0:T(8,128)S(1)} %copy-done.1), custom_call_target="tpu_custom_call" | custom-call | flops 300000000 | bytes 4194304 | tf_op jit(solution)/shard_map/pallas_call | solution.py:406
  120.3 0.6 copy.12
  (3 shorter events, 0.0 us)
Async XLA Ops:
  0.0 91.2 %copy-start.2 = (s32[2]{0:T(128)S(1)}, s32[2]{0:T(128)}, u32[]{:S(2)}) copy-start(s32[2]{0:T(128)} %param.12) | copy-start | bytes 28
  0.0 91.4 %copy-start = (bf16[512,2048]{1,0:T(8,128)(2,1)S(1)}, bf16[512,2048]{1,0:T(8,128)(2,1)}, u32[]{:S(2)}) copy-start(bf16[512,2048]{1,0:T(8,128)(2,1)} %index_ref.1) | copy-start | bytes 6291460
  0.0 91.4 %copy-start.1 = (s32[64,64]{1,0:T(8,128)S(1)}, s32[64,64]{1,0:T(8,128)}, u32[]{:S(2)}) copy-start(s32[64,64]{1,0:T(8,128)} %cand_ref.1) | copy-start | bytes 49156

commit v2 on v0

v2 whole, which is shorter than its diff:
```python
import functools

import jax
import jax.numpy as jnp
from jax import lax
from jax.experimental import pallas as pl
from jax.experimental.pallas import tpu as pltpu
from jax.sharding import PartitionSpec as P

HEAD = 64
MESH = pl.DeviceIdType.MESH
F32 = jnp.float32
BF16 = jnp.bfloat16


def grid_of(count):
    chips = count // 2
    side = 4 if chips >= 64 else 2
    return chips // (side * side), side, side


def split_rows(value):
    high = value.astype(BF16)
    low = (value - high.astype(F32)).astype(BF16)
    return jnp.concatenate([high, low], axis=0)


def kernel(
    count, lengths_ref, order_ref, hidden_hbm, gain_ref, wq_hbm, wk_hbm, wv_hbm, wo_hbm,
    index_hbm, cand_ref, out_ref,
    hidden_ref, normed_ref, gq, gk, gv, go, q_ref, k_ref, psum_ref, index_ref,
    context_mine, context_got, context_flat, part_mine, part_got,
    rows_ref, note_ref, got, mine, back,
    send, recv, local, send_o, recv_o, send_c, recv_c, send_p, recv_p,
    send_n, recv_n, send_s, recv_s,
):
    planes, rows, cols = grid_of(count)
    plane = rows * cols * 2
    me = lax.axis_index("dp")
    core = lax.rem(me, 2)
    b = lax.rem(me // 2, cols)
    a = lax.rem(me // (2 * cols), rows)
    z = me // plane
    place = lax.rem(me, plane)
    texts = lengths_ref.shape[0]
    slots, width = hidden_ref.shape
    lmax = slots // texts
    features = q_ref.shape[1]
    heads = features // HEAD
    span = 256

    def device(zz, aa, bb, cc):
        return ((zz * rows + aa) * cols + bb) * 2 + cc

    def others(size, own):
        return [lax.rem(own + step, size) for step in range(1, size)]

    z_line = [device(o, a, b, core) for o in others(planes, z)]
    a_line = [device(z, o, b, core) for o in others(rows, a)]
    b_line = [device(z, a, o, core) for o in others(cols, b)]
    twin = device(z, a, b, 1 - core)

    hidden_copy = pltpu.make_async_copy(hidden_hbm, hidden_ref, local.at[0])
    hidden_copy.start()

    pieces = []
    for start in range(0, features, span):
        pieces += [(wq_hbm, gq, start), (wk_hbm, gk, start)]
    for start in range(0, features, span):
        pieces += [(wv_hbm, gv, start)]
    blocks = features // span

    local_copies = []
    for i, (source, held, start) in enumerate(pieces):
        copy = pltpu.make_async_copy(
            source.at[:, pl.ds(start, span)],
            held.at[z, a, b, core, :, pl.ds(start, span)],
            local.at[3 + i],
        )
        copy.start()
        local_copies.append(copy)

    barrier = pltpu.get_barrier_semaphore()

    @pl.loop(1, count)
    def _(step):
        pl.semaphore_signal(
            barrier, inc=1, device_id=(lax.rem(me + step, count),), device_id_type=MESH
        )

    pl.semaphore_wait(barrier, count - 1)

    def remote(src, dst, send_sem, recv_sem, target):
        return pltpu.make_async_remote_copy(
            src_ref=src, dst_ref=dst, send_sem=send_sem, recv_sem=recv_sem,
            device_id=(target,), device_id_type=MESH,
        )

    stages = []
    for i, (source, held, start) in enumerate(pieces):
        half = span // 2
        first, second = pl.ds(start, half), pl.ds(start + half, half)
        whole = pl.ds(start, span)
        ends = []
        ends += [(0, source.at[:, whole], held.at[z, a, b, core, :, whole], t) for t in z_line]
        part = held.at[:, a, b, core, :, first]
        ends += [(1, part, part, t) for t in b_line]
        part = held.at[:, a, b, core, :, second]
        ends += [(1, part, part, t) for t in a_line]
        part = held.at[:, a, :, core, :, first]
        ends += [(2, part, part, t) for t in a_line]
        part = held.at[:, :, b, core, :, second]
        ends += [(2, part, part, t) for t in b_line]
        part = held.at[:, :, :, core, :, whole]
        ends += [(3, part, part, twin)]
        plan = ([], [], [], [])
        for slot, (stage, src, dst, target) in enumerate(ends):
            plan[stage].append(remote(src, dst, send.at[i, slot], recv.at[i, slot], target))
        stages.append(plan)

    def begin(piece, stage):
        if 0 <= piece < len(pieces):
            if stage == 1:
                local_copies[piece].wait()
            for copy in stages[piece][stage]:
                copy.start()

    def finish(piece, stage):
        if 0 <= piece < len(pieces):
            for copy in stages[piece][stage]:
                copy.wait()

    def advance(step):
        finish(step, 0)
        begin(step, 1)
        begin(step + 3, 0)
        finish(step - 1, 1)
        begin(step - 1, 2)
        finish(step - 2, 2)
        begin(step - 2, 3)
        finish(step - 3, 3)

    def norm_rows():
        tile = 128

        @pl.loop(0, slots // tile)
        def _(i):
            at = pl.ds(pl.multiple_of(i * tile, tile), tile)
            x = hidden_ref[at, :].astype(F32)
            mean = jnp.mean(x * x, axis=-1, keepdims=True)
            normed_ref[at, :] = (x * lax.rsqrt(mean + 1e-06) * gain_ref[...]).astype(BF16)

    def project(held, out, c):
        tile = 512

        @pl.loop(0, slots // tile)
        def _(i):
            at = pl.ds(pl.multiple_of(i * tile, tile), tile)
            w = held[:, :, :, :, :, c:c + span].reshape(width, span)
            out[at, c:c + span] = jnp.dot(
                normed_ref[at, :], w, preferred_element_type=F32
            ).astype(BF16)

    def attend(pair):
        lane = lax.broadcasted_iota(jnp.int32, (1, 2 * HEAD), 1)
        key_slot = lax.broadcasted_iota(jnp.int32, (1, lmax), 1)
        query_slot = lax.broadcasted_iota(jnp.int32, (lmax, 1), 0)
        at = pl.ds(pair * 2 * HEAD, 2 * HEAD)

        @pl.loop(0, texts)
        def _(t):
            length = lengths_ref[t]
            key_valid = key_slot < length
            query_valid = query_slot < length
            mine_rows = pl.ds(pl.multiple_of(t * lmax, lmax), lmax)
            q = q_ref[mine_rows, at]
            k = k_ref[mine_rows, at]
            for side in range(2):
                q_one = jnp.where((lane // HEAD) == side, q, jnp.zeros_like(q))
                logits = lax.dot_general(
                    q_one, k, (((1,), (1,)), ((), ())), preferred_element_type=F32
                )
                logits = jnp.where(key_valid, logits, F32(-1e30))
                top = jnp.max(logits, axis=1, keepdims=True)
                e = jnp.exp(logits - top)
                weight = jnp.where(
                    query_valid, 1.0 / jnp.sum(e, axis=1, keepdims=True), F32(0.0)
                )
                psum_ref[t, pair:pair + 1, side * lmax:(side + 1) * lmax] = jnp.sum(
                    e * weight, axis=0, keepdims=True
                )

    def combine():
        combined = []
        for t in range(texts):
            both = jnp.concatenate(
                [psum_ref[t, :, 0:lmax], psum_ref[t, :, lmax:2 * lmax]], axis=0
            )
            part = jnp.dot(
                split_rows(both), normed_ref[t * lmax:(t + 1) * lmax, :],
                preferred_element_type=F32,
            )
            combined.append(part[0:heads] + part[heads:2 * heads])
        return split_rows(jnp.concatenate(combined, axis=0))

    def value_piece(stacked, c):
        lane = c + lax.broadcasted_iota(jnp.int32, (heads, span), 1)
        row = lax.broadcasted_iota(jnp.int32, (heads, span), 0)
        head = jnp.where(row < heads // 2, 2 * row, 2 * (row - heads // 2) + 1)
        w = gv[:, :, :, :, :, c:c + span].reshape(width, span)
        spread = jnp.dot(stacked, w, preferred_element_type=F32)
        spread = spread[0:texts * heads] + spread[texts * heads:2 * texts * heads]
        for t in range(texts):
            context_mine[t:t + 1, c:c + span] = jnp.sum(
                jnp.where(lane // HEAD == head, spread[t * heads:(t + 1) * heads], F32(0.0)),
                axis=0, keepdims=True,
            )

    for piece in range(3):
        begin(piece, 0)
    out_local = pltpu.make_async_copy(wo_hbm, go.at[z], local.at[1])
    out_local.start()
    index_copy = pltpu.make_async_copy(index_hbm, index_ref, local.at[2])
    index_copy.start()
    out_copies = [
        remote(wo_hbm, go.at[z], send_o.at[i], recv_o.at[i], target)
        for i, target in enumerate(z_line)
    ]
    hidden_copy.wait()
    norm_rows()

    pairs = heads // 2
    done = 0
    stacked = None
    for step in range(len(pieces) + 3):
        advance(step)
        ready = step - 3
        if ready == 0:
            for copy in out_copies:
                copy.start()
        if 0 <= ready < 2 * blocks:
            if ready % 2 == 0:
                project(gq, q_ref, (ready // 2) * span)
            else:
                project(gk, k_ref, (ready // 2) * span)
        if 1 <= ready < 2 * blocks:
            attend(done)
            done += 1
        if ready == 2 * blocks:
            while done < pairs:
                attend(done)
                done += 1
            stacked = combine()
        if ready >= 2 * blocks:
            value_piece(stacked, (ready - 2 * blocks) * span)

    def plane_device(step):
        return z * plane + lax.rem(place + step, plane)

    def plane_source(step):
        return lax.rem(place + plane - step, plane)

    def context_copy(step):
        return remote(
            context_mine, context_got.at[place], send_c.at[step], recv_c.at[step],
            plane_device(step),
        )

    for step in range(1, plane):
        context_copy(step).start()
    context_got[place] = context_mine[...]
    out_local.wait()
    for copy in out_copies:
        copy.wait()
    rows_out = go.shape[1]
    depth = planes * rows_out
    feature = lax.broadcasted_iota(jnp.int32, (features, depth), 0)
    slot = lax.broadcasted_iota(jnp.int32, (features, depth), 1)
    wanted = (slot // rows_out) * (plane * rows_out) + place * rows_out + lax.rem(slot, rows_out)
    choose = jnp.where(feature == wanted, 1.0, 0.0).astype(BF16)
    key_slot = lax.broadcasted_iota(jnp.int32, (16, lmax), 1)
    totals = []
    for t in range(texts):
        valid = jnp.where(key_slot < lengths_ref[t], 1.0, 0.0).astype(BF16)
        totals.append(
            jnp.dot(
                valid, hidden_ref[t * lmax:(t + 1) * lmax, :], preferred_element_type=F32
            )[0:1]
        )
    for step in range(1, plane):
        remote(
            context_mine, context_got.at[plane_source(step)], send_c.at[step],
            recv_c.at[step], plane_device(step),
        ).wait()
    for j in range(plane):
        context_flat[j * texts:(j + 1) * texts, :] = context_got[j]
    group = plane * texts
    chosen = jnp.dot(split_rows(context_flat[...]), choose, preferred_element_type=F32)
    held_out = go[...].reshape(depth, width).astype(BF16)
    part = jnp.dot(chosen.astype(BF16), held_out, preferred_element_type=F32)
    part = part[0:group] + part[group:2 * group]
    for j in range(plane):
        part_mine[j] = part[j * texts:(j + 1) * texts, :]

    def part_copy(step, where):
        return remote(
            part_mine.at[lax.rem(place + step, plane)], part_got.at[where], send_p.at[step],
            recv_p.at[step], plane_device(step),
        )

    for step in range(1, plane):
        part_copy(step, place).start()
    part_got[place] = part_mine[place]
    for step in range(1, plane):
        part_copy(step, plane_source(step)).wait()
    summed = part_got[0]
    for j in range(1, plane):
        summed += part_got[j]
    wide = width // 8
    for t in range(texts):
        pooled = (totals[t] + summed[t:t + 1]) / lengths_ref[t].astype(F32)
        mean = jnp.mean(pooled * pooled, axis=-1, keepdims=True)
        unit = pooled * lax.rsqrt(mean + 1e-06)
        for k in range(8):
            rows_ref[t * 8 + k:t * 8 + k + 1, 0:wide] = unit[:, k * wide:(k + 1) * wide]
        rows_ref[t * 8:(t + 1) * 8, wide:wide + 128] = jnp.full(
            (8, 128), order_ref[t], jnp.int32
        ).astype(F32)
    note_ref[...] = rows_ref[...].astype(BF16)

    line = [
        remote(note_ref, got.at[z, place], send_n.at[i], recv_n.at[i], target)
        for i, target in enumerate(z_line)
    ]
    for copy in line:
        copy.start()
    got[z, place] = note_ref[...]
    for copy in line:
        copy.wait()

    def note_copy(step, where):
        return remote(
            got.at[:, where], got.at[:, where], send_n.at[planes - 1 + step],
            recv_n.at[planes - 1 + step], plane_device(step),
        )

    for step in range(1, plane):
        note_copy(step, place).start()
    index_copy.wait()
    for step in range(1, plane):
        note_copy(step, place).wait_send()
        note_copy(step, plane_source(step)).wait_recv()

    total = count * texts
    rows_dev = index_ref.shape[0]
    long = count * texts * 8
    flat = got[...].reshape(long, wide + 128)
    data = flat[:, 0:wide]
    numbers = flat[:, wide:wide + 128].astype(F32).T[0:1, :].astype(jnp.int32)
    lane = lax.broadcasted_iota(jnp.int32, (total, long), 1)
    row = lax.broadcasted_iota(jnp.int32, (total, long), 0)
    same = numbers == row
    scores = jnp.zeros((total, rows_dev), F32)
    for k in range(8):
        pick = jnp.where(same & (lax.rem(lane, 8) == k), 1.0, 0.0).astype(BF16)
        unit = jnp.dot(pick, data, preferred_element_type=F32).astype(BF16)
        scores += lax.dot_general(
            unit, index_ref[:, k * wide:(k + 1) * wide], (((1,), (1,)), ((), ())),
            preferred_element_type=F32,
        )
    within = cand_ref[...] - me * rows_dev
    slot = lax.broadcasted_iota(jnp.int32, (1, 1, rows_dev), 2)
    for r in range(0, total, 8):
        hit = within[r:r + 8][:, :, None] == slot
        found = jnp.sum(jnp.where(hit, scores[r:r + 8][:, None, :], F32(0.0)), axis=2)
        for j in range(0, 8, texts):
            mine[(r + j) // texts] = found[j:j + texts, :]

    def back_copy(step, where):
        target = lax.rem(me + step, count)
        return remote(
            mine.at[target], back.at[where], send_s.at[step], recv_s.at[step], target
        )

    @pl.loop(1, count)
    def _(step):
        back_copy(step, me).start()

    back[me] = mine[me]

    @pl.loop(1, count)
    def _(step):
        back_copy(step, lax.rem(me + count - step, count)).wait()

    out_ref[...] = jnp.sum(back[...], axis=0)


def solution(mesh):
    count = mesh.shape["dp"]
    planes, rows, cols = grid_of(count)
    plane = rows * cols * 2

    def per_device(
        hidden, lengths, order, candidates, norm_gain, w_query, w_key, w_value, w_out, index_rows
    ):
        texts, lmax, width = hidden.shape
        slots, features = texts * lmax, w_query.shape[1]
        if w_out.shape[0] % 16:
            w_out = w_out.astype(F32)
        cand = candidates.shape[1]
        lead = (planes, rows, cols, 2)
        held = pltpu.VMEM(lead + w_query.shape, BF16)
        copies = planes - 1 + 2 * (rows - 1 + cols - 1) + 1
        pieces = 3 * features // 256
        note = (texts * 8, width // 8 + 128)
        dma = pltpu.SemaphoreType.DMA
        anywhere = pl.BlockSpec(memory_space=pl.ANY)
        scalar = pl.BlockSpec(memory_space=pltpu.SMEM)
        vector = pl.BlockSpec(memory_space=pltpu.VMEM)
        return pl.pallas_call(
            functools.partial(kernel, count),
            out_shape=jax.ShapeDtypeStruct((texts, cand), F32),
            in_specs=[scalar, scalar, anywhere, vector] + [anywhere] * 5 + [vector],
            out_specs=vector,
            scratch_shapes=[
                pltpu.VMEM((slots, width), BF16),
                pltpu.VMEM((slots, width), BF16),
                held, held, held,
                pltpu.VMEM((planes,) + w_out.shape, w_out.dtype),
                pltpu.VMEM((slots, features), BF16),
                pltpu.VMEM((slots, features), BF16),
                pltpu.VMEM((texts, features // HEAD // 2, 2 * lmax), F32),
                pltpu.VMEM(index_rows.shape, BF16),
                pltpu.VMEM((texts, features), F32),
                pltpu.VMEM((plane, texts, features), F32),
                pltpu.VMEM((plane * texts, features), F32),
                pltpu.VMEM((plane, texts, width), F32),
                pltpu.VMEM((plane, texts, width), F32),
                pltpu.VMEM(note, F32),
                pltpu.VMEM(note, BF16),
                pltpu.VMEM((planes, plane) + note, BF16),
                pltpu.VMEM((count, texts, cand), F32),
                pltpu.VMEM((count, texts, cand), F32),
                dma((pieces, copies)), dma((pieces, copies)), dma((pieces + 3,)),
                dma((planes,)), dma((planes,)), dma((plane,)), dma((plane,)),
                dma((plane,)), dma((plane,)), dma((planes + plane,)), dma((planes + plane,)),
                dma((count,)), dma((count,)),
            ],
            compiler_params=pltpu.CompilerParams(
                collective_id=0, has_side_effects=True, vmem_limit_bytes=56 * 1024 * 1024
            ),
            cost_estimate=pl.CostEstimate(
                flops=10 ** 10, bytes_accessed=24 * 2 ** 20, transcendentals=2 ** 23
            ),
        )(
            lengths, order, hidden.reshape(slots, width), norm_gain.reshape(1, width),
            w_query, w_key, w_value, w_out, index_rows, candidates,
        )

    return jax.shard_map(
        per_device,
        mesh=mesh,
        in_specs=(
            P("dp", None, None),
            P("dp"),
            P("dp"),
            P(),
            P(),
            P("dp", None),
            P("dp", None),
            P("dp", None),
            P("dp", None),
            P("dp", None),
        ),
        out_specs=P("dp", None),
        check_vma=False,
    )
```

time: 440 us -> 104 us (0.24)
  blocking collectives: 159 us -> 0 us
  Pallas kernels: 0 us -> 103 us
  waiting for transfers between devices: 95.5 us -> 0 us
  local copies, waits for them, and re-layouts: 78.3 us -> 1.24 us
  matrix products: 77 us -> 0 us
  other arithmetic: 15.3 us -> 0 us
  between operations: 13.3 us -> 0.01 us
    pallas_call x0 -> x1, Pallas kernels: none -> 103 us  [per_device(): pl.pallas_call(functools.partial(kernel, count), out_shape=jax.ShapeDtype...]
    all_gather x4 -> x0, waiting for transfers between devices: 92.9 us -> none  [the longest x1 42.4 us: per_device(): lax.all_gather(w_key, 'dp', axis=0, tiled=True)]
    all_gather x2 -> x0, blocking collectives: 80 us -> none  [the longest x1 40.2 us: per_device(): every_score = lax.all_gather(mine, 'dp', axis=0, tiled=True)]
    unnamed x2 -> x0, blocking collectives: 79.3 us -> none
    dot_general x7 -> x0, matrix products: 55.4 us -> none  [the longest x2 17.6 us: attend_text(): jnp.einsum('hqk,khd->qhd', probs, value_side, preferred_element_type=jnp....]
    gather x5 -> x0, local copies, waits for them, and re-layouts: 35.3 us -> none  [the longest x3 33.5 us: per_device(): jnp.take_along_axis(local_scores, jnp.clip(within, 0, rows_dev - 1), axis=1)]
    sub x2 -> x0, matrix products: 21.5 us -> none  [attend_text(): probs = jax.nn.softmax(logits, axis=-1).astype(jnp.bfloat16)]
    while x4 -> x0, local copies, waits for them, and re-layouts: 20.1 us -> none  [per_device(): lax.map(attend_text, (queries, key_side, value_side, lengths))]
  transfers between devices with their start and end apart: 4 -> 0, of which waited for: 3 -> 0; matrix products, arithmetic and copies ran while one was open for 29% -> 0% of each run, Pallas kernels for 0% -> 0%
where the time goes in v2:
time: 104 us
  Pallas kernels  103 us (99%)
  local copies, waits for them, and re-layouts  1.24 us (1%)
    pallas_call x1, Pallas kernels, per_device(): pl.pallas_call(functools.partial(kernel, count), out_shape=jax.ShapeDtype...  103 us

profile of v2, /device:TPU:0, one launch (start us, length us, event | category | flops | bytes accessed | tf_op | source)
XLA Modules:
  0.0 103.9 jit_solution(7957647994571123851)
XLA Ops:
  0.0 102.6 %shard_map.100 = f32[2,64]{1,0:T(2,128)} custom-call(s32[2]{0:T(128)} %lengths_ref.1, s32[2]{0:T(128)} %order_ref.1, bf16[1024,2048]{1,0:T(8,128)(2,1)} %bitcast.2, f32[1,2048]{1,0:T(1,128)} %bitcast.3, bf16[64,1024]{1,0:T(8,128)(2,1)} %wq_hbm.1, bf16[64,1024]{1,0:T(8,128)(2,1)} %wk_hbm.1, bf16[64,1024]{1,0:T(8,128)(2,1)} %wv_hbm.1, ...), custom_call_target="tpu_custom_call" | custom-call | flops 10000000000 | bytes 25165824 | tf_op jit(solution)/shard_map/pallas_call | solution.py:420
  102.6 1.2 %copy.12 = f32[2,64]{1,0:T(2,128)} copy(f32[2,64]{1,0:T(2,128)} %shard_map.100) | data formatting | bytes 1024

commit v3 on v2

--- a/solution.py
+++ b/solution.py
@@ -161,34 +161,28 @@
                 normed_ref[at, :], w, preferred_element_type=F32
             ).astype(BF16)
 
-    def attend(pair):
+    def attend(pair, t):
         lane = lax.broadcasted_iota(jnp.int32, (1, 2 * HEAD), 1)
-        key_slot = lax.broadcasted_iota(jnp.int32, (1, lmax), 1)
-        query_slot = lax.broadcasted_iota(jnp.int32, (lmax, 1), 0)
+        slot = lax.broadcasted_iota(jnp.int32, (lmax, 1), 0)
+        valid = slot < lengths_ref[t]
+        mask = jnp.where(valid, 0.0, -1e30).astype(BF16)
         at = pl.ds(pair * 2 * HEAD, 2 * HEAD)
-
-        @pl.loop(0, texts)
-        def _(t):
-            length = lengths_ref[t]
-            key_valid = key_slot < length
-            query_valid = query_slot < length
-            mine_rows = pl.ds(pl.multiple_of(t * lmax, lmax), lmax)
-            q = q_ref[mine_rows, at]
-            k = k_ref[mine_rows, at]
-            for side in range(2):
-                q_one = jnp.where((lane // HEAD) == side, q, jnp.zeros_like(q))
-                logits = lax.dot_general(
-                    q_one, k, (((1,), (1,)), ((), ())), preferred_element_type=F32
-                )
-                logits = jnp.where(key_valid, logits, F32(-1e30))
-                top = jnp.max(logits, axis=1, keepdims=True)
-                e = jnp.exp(logits - top)
-                weight = jnp.where(
-                    query_valid, 1.0 / jnp.sum(e, axis=1, keepdims=True), F32(0.0)
-                )
-                psum_ref[t, pair:pair + 1, side * lmax:(side + 1) * lmax] = jnp.sum(
-                    e * weight, axis=0, keepdims=True
-                )
+        q = q_ref[t * lmax:(t + 1) * lmax, at]
+        k = k_ref[t * lmax:(t + 1) * lmax, at]
+        for side in range(2):
+            spare = (1 - side) * HEAD
+            unit = jnp.where(lane == spare, 1.0, 0.0).astype(BF16)
+            q_one = jnp.where((lane // HEAD) == side, q, unit)
+            k_one = jnp.where(lane == spare, mask, k)
+            logits = lax.dot_general(
+                q_one, k_one, (((1,), (1,)), ((), ())), preferred_element_type=F32
+            )
+            top = jnp.max(logits, axis=1, keepdims=True)
+            e = jnp.exp(logits - top)
+            weight = jnp.where(valid, 1.0 / jnp.sum(e, axis=1, keepdims=True), F32(0.0))
+            psum_ref[t, pair:pair + 1, side * lmax:(side + 1) * lmax] = jnp.sum(
+                e * weight, axis=0, keepdims=True
+            )
 
     def combine():
         combined = []
@@ -229,30 +223,41 @@
     hidden_copy.wait()
     norm_rows()
 
-    pairs = heads // 2
-    done = 0
-    stacked = None
-    for step in range(len(pieces) + 3):
-        advance(step)
-        ready = step - 3
-        if ready == 0:
-            for copy in out_copies:
-                copy.start()
-        if 0 <= ready < 2 * blocks:
-            if ready % 2 == 0:
-                project(gq, q_ref, (ready // 2) * span)
-            else:
-                project(gk, k_ref, (ready // 2) * span)
-        if 1 <= ready < 2 * blocks:
-            attend(done)
-            done += 1
-        if ready == 2 * blocks:
-            while done < pairs:
-                attend(done)
-                done += 1
-            stacked = combine()
-        if ready >= 2 * blocks:
-            value_piece(stacked, (ready - 2 * blocks) * span)
+    units = []
+    waiting = []
+    per_block = span // (2 * HEAD)
+    for block in range(blocks):
+        c = block * span
+        units.append((2 * block, 2.5, functools.partial(project, gq, q_ref, c)))
+        units += waiting[:2]
+        waiting = waiting[2:]
+        units.append((2 * block + 1, 2.5, functools.partial(project, gk, k_ref, c)))
+        for pair in range(block * per_block, (block + 1) * per_block):
+            for t in range(texts):
+                waiting.append((2 * block + 1, 1.5, functools.partial(attend, pair, t)))
+        units += waiting[:2]
+        waiting = waiting[2:]
+    units += waiting
+    steps = len(pieces) + 3
+    pace, clock, step = 4.2, 0.0, 0
+    while units:
+        if step < steps and (units[0][0] > step - 4 or clock >= pace * (step + 1)):
+            advance(step)
+            if step == 3:
+                for copy in out_copies:
+                    copy.start()
+            step += 1
+            clock = max(clock, pace * step)
+        else:
+            _, cost, run = units.pop(0)
+            run()
+            clock += cost
+    stacked = combine()
+    for block in range(blocks):
+        while step < steps and step - 4 < 2 * blocks + block:
+            advance(step)
+            step += 1
+        value_piece(stacked, block * span)
 
     def plane_device(step):
         return z * plane + lax.rem(place + step, plane)

time: 104 us -> 104 us (level)
  no operation moved by 1% of the time
where the time goes in v3:
time: 104 us
  Pallas kernels  103 us (99%)
  local copies, waits for them, and re-layouts  1.24 us (1%)
    pallas_call x1, Pallas kernels, per_device(): pl.pallas_call(functools.partial(kernel, count), out_shape=jax.ShapeDtype...  103 us

profile of v3, /device:TPU:0, one launch (start us, length us, event | category | flops | bytes accessed | tf_op | source)
XLA Modules:
  0.0 104.0 jit_solution(287404044507517052)
XLA Ops:
  0.0 102.7 %shard_map.100 = f32[2,64]{1,0:T(2,128)} custom-call(s32[2]{0:T(128)} %lengths_ref.1, s32[2]{0:T(128)} %order_ref.1, bf16[1024,2048]{1,0:T(8,128)(2,1)} %bitcast.2, f32[1,2048]{1,0:T(1,128)} %bitcast.3, bf16[64,1024]{1,0:T(8,128)(2,1)} %wq_hbm.1, bf16[64,1024]{1,0:T(8,128)(2,1)} %wk_hbm.1, bf16[64,1024]{1,0:T(8,128)(2,1)} %wv_hbm.1, ...), custom_call_target="tpu_custom_call" | custom-call | flops 10000000000 | bytes 25165824 | tf_op jit(solution)/shard_map/pallas_call | solution.py:425
  102.7 1.2 %copy.12 = f32[2,64]{1,0:T(2,128)} copy(f32[2,64]{1,0:T(2,128)} %shard_map.100) | data formatting | bytes 1024
